TPU v7x, 32 devices: a whole 2x2x4 slice. The times are simulated.
32 devices in a mesh: grp: 4 (over y, x), dev: 8 (over z, core).
Axes of the slice: x: 2, y: 2, z: 4, core: 2. Of those that a mesh axis runs over, the one named last changes fastest.
Arguments:
- state: float32 [2, 8, 131072], P(None, None, ('grp', 'dev')), may hold values from -6 to 6
- gates: float32 [2, 4, 2, 128, 128], replicated, may hold values from -0.375 to 0.375
- local_perm: int32 [2, 12], replicated, may hold values from 0 to 11, each once within a row
Outputs:
- final_state: float32 [2, 8, 131072], P(None, None, ('grp', 'dev'))
Inputs may be any that keep to these rules, and one draw needn't show every extreme that they name: Each row of local_perm names each of the 12 local qubits once.
All inputs are finite; a program needn't handle non-finite values.
Results may differ from a plain program's by a relative error of at most 0.0001.
Values sent between devices are 32-bit elements; how exact they have to be, the bound alone decides.
A program may use at most 64 MiB of HBM per device.

v0:
```python
import functools

import jax
import jax.numpy as jnp
from jax import lax
from jax.experimental import pallas as pl
from jax.experimental.pallas import tpu as pltpu
from jax.sharding import PartitionSpec as P

MESH = pl.DeviceIdType.MESH
CYCLES = 2
GATES = 4


def permutation_plan(perm, nbits, gate_bits, lane):
    row_bits = nbits - gate_bits
    shared = gate_bits - row_bits
    leaving = sum(1 << perm[b] for b in range(gate_bits, nbits))
    enters = [1 - (leaving >> (gate_bits + j) & 1) for j in range(row_bits)]
    open_slots = closed_slots = 0
    open_at = closed_at = 0
    for j in range(gate_bits):
        is_open = enters[j] if j < row_bits else 0
        open_slots = open_slots + (j * is_open << open_at)
        closed_slots = closed_slots + (j * (1 - is_open) << closed_at)
        open_at = open_at + 4 * is_open
        closed_at = closed_at + 4 * (1 - is_open)
    slot = []
    position_low = position_high = 0
    for q in range(gate_bits):
        leaves = leaving >> q & 1
        here = jnp.where(leaves == 1, open_slots, closed_slots) & 15
        open_slots = open_slots >> 4 * leaves
        closed_slots = closed_slots >> 4 * (1 - leaves)
        slot.append(here)
        position_low = position_low + (here + gate_bits * leaves << 4 * q)
    for j in range(row_bits):
        position_high = position_high + (gate_bits + j - gate_bits * enters[j] << 4 * j)
    placed = []
    for b in range(nbits):
        low = position_low >> 4 * jnp.minimum(perm[b], gate_bits - 1) & 15
        high = position_high >> 4 * jnp.maximum(perm[b] - gate_bits, 0) & 15
        placed.append(jnp.where(perm[b] < gate_bits, low, high))

    def lane_map(places):
        return sum((lane >> k & 1) << place for k, place in enumerate(places))

    high_place = list(range(row_bits, gate_bits)) + [place - gate_bits for place in placed[gate_bits:]]
    maps = [lane_map(slot), lane_map(placed[:gate_bits]), lane_map(high_place)]
    return maps, [enter == 1 for enter in enters]


def split(x):
    high = x.astype(jnp.bfloat16)
    low = (x - high.astype(jnp.float32)).astype(jnp.bfloat16)
    return high, low


def dot(a, b, contract):
    return lax.dot_general(a, b, (contract, ((), ())), preferred_element_type=jnp.float32)


NT = ((1,), (1,))
NN = ((1,), (0,))


def swap_lane_bit(first, second, bit, lane, condition=None):
    width = first.shape[-1]
    axis = first.ndim - 1
    up = (lane >> bit & 1) == 1
    down = ~up
    if condition is not None:
        up = up & condition
        down = down & condition
    new_first = jnp.where(up, pltpu.roll(second, 1 << bit, axis), first)
    new_second = jnp.where(down, pltpu.roll(first, width - (1 << bit), axis), second)
    return new_first, new_second


def one_hot(lane_map):
    width = lane_map.shape[-1]
    rows = lax.broadcasted_iota(jnp.int32, (width, width), 0)
    return jnp.where(rows == lane_map, 1.0, 0.0).astype(jnp.bfloat16)


def gate_matrix(real, imag, columns):
    width = real.shape[-1]
    re_high, re_low = split(real)
    im_high, im_low = split(imag)
    if columns is not None:
        stack = jnp.concatenate([re_high, re_low, im_high, im_low])
        moved = dot(stack, columns, NT).astype(jnp.bfloat16)
        re_high, re_low, im_high, im_low = [moved[i * width : (i + 1) * width] for i in range(4)]

    def whole(re, im):
        return jnp.concatenate(
            [jnp.concatenate([re, -im], axis=1), jnp.concatenate([im, re], axis=1)], axis=0
        )

    return whole(re_high, im_high), whole(re_low, im_low)


def kernel(
    sizes,
    state_hbm,
    gates_hbm,
    perm_hbm,
    out_ref,
    state_ref,
    gates_ref,
    perm_ref,
    work,
    sent,
    landed,
    send_sem,
    recv_sem,
    load_sem,
):
    traj, nbits, gate_bits, grp_bits, dev_bits = sizes
    width = 1 << gate_bits
    row_bits = nbits - gate_bits
    shared = gate_bits - row_bits
    rows = 1 << row_bits
    blocks = 1 << dev_bits
    top = blocks // 2
    wide = dev_bits > row_bits
    grp = lax.axis_index("grp")
    dev = lax.axis_index("dev")
    grp_low = grp % 2
    grp_next = grp // 2 % 2
    grp_rest = grp // 4 * 4
    dev_top = dev // top
    dev_low = dev % top

    def targets(cycle, step):
        low = (dev_low ^ (step % top)) if step % top else dev_low
        high = 1 - grp_next if step // top else grp_next
        block = high * top + low
        if cycle == 0:
            return block, grp_rest + high * 2 + grp_low, grp_next * top + low, dev
        return block, grp_rest + high * 2 + grp_next, dev_top * top + low, grp_low * top + dev_low

    self_sent = [dev_top == grp_next, grp_low == grp_next]

    barrier = pltpu.get_barrier_semaphore()
    for step in range(blocks):
        low = (dev_low ^ (step % top)) if step % top else dev_low
        high = step // top
        source_high = 1 - dev_top if high else dev_top
        first = (grp_rest + dev_top * 2 + grp_low, source_high * top + low)
        source_low = 1 - grp_low if high else grp_low
        second = (grp_rest + grp_low * 2 + source_low, dev_top * top + low)

        def tell(device):
            pl.semaphore_signal(barrier, inc=1, device_id=device, device_id_type=MESH)

        if step:
            tell(first)
            tell(second)
        else:
            pl.when(dev_top != grp_next)(functools.partial(tell, first))
            pl.when(grp_low != grp_next)(functools.partial(tell, second))

    loads = [
        pltpu.make_async_copy(perm_hbm, perm_ref, load_sem.at[0]),
        pltpu.make_async_copy(state_hbm, state_ref, load_sem.at[1]),
    ]
    for cycle in range(CYCLES):
        for which in range(GATES):
            sem = load_sem.at[2 + GATES * cycle + which]
            loads.append(
                pltpu.make_async_copy(gates_hbm.at[cycle, which], gates_ref.at[cycle, which], sem)
            )
    for load in loads:
        load.start()

    lane = lax.broadcasted_iota(jnp.int32, (1, width), 1)
    fixed = one_hot((lane % (1 << shared)) * rows + lane // (1 << shared))

    def low_matrix(cycle, which, lane_map):
        columns = None if lane_map is None else one_hot(lane_map)
        loads[2 + GATES * cycle + which].wait()
        return gate_matrix(gates_ref[cycle, which, 0], gates_ref[cycle, which, 1], columns)

    def high_matrix(cycle, which, columns):
        parts = []
        loads[2 + GATES * cycle + which].wait()
        for part in range(2):
            parts.append(
                jnp.concatenate(
                    [
                        gates_ref[cycle, which, part, pl.ds(a, rows, stride=1 << shared), :]
                        for a in range(1 << shared)
                    ]
                )
            )
        return gate_matrix(parts[0], parts[1], columns)

    def apply_low(x, matrix):
        high, low = split(jnp.concatenate([x[0], x[1]], axis=1))
        m_high, m_low = matrix
        y = dot(high, m_high, NT) + (dot(low, m_high, NT) + dot(high, m_low, NT))
        return y[:, :width], y[:, width:]

    def swap_traj(planes):
        planes = list(planes)
        for bit in range(shared):
            for t in range(len(planes)):
                if not t >> bit & 1:
                    o = t | 1 << bit
                    planes[t], planes[o] = swap_lane_bit(planes[t], planes[o], row_bits + bit, lane)
        return planes

    def apply_high(source, matrix, write):
        per = 1 << shared
        operand = []
        for part in range(2):
            planes = [source[part, pl.ds(t, rows, stride=traj), :] for t in range(traj)]
            planes = swap_traj(planes)
            operand.append(
                jnp.concatenate(
                    [jnp.concatenate(planes[g : g + per], axis=0) for g in range(0, traj, per)], axis=1
                )
            )
        high, low = split(jnp.concatenate(operand, axis=0))
        m_high, m_low = matrix
        y = dot(m_high, high, NN) + (dot(m_low, high, NN) + dot(m_high, low, NN))
        for part in range(2):
            planes = [
                y[part * width + a * rows : part * width + (a + 1) * rows, g * width : (g + 1) * width]
                for g in range(traj // per)
                for a in range(per)
            ]
            planes = swap_traj(planes)
            for t in range(traj):
                write[part, pl.ds(t, rows, stride=traj), :] = planes[t]

    def local_part(x, plan, cycle, matrices):
        maps, conditions = plan
        lanes = one_hot(maps[0])
        moved = []
        for part in range(2):
            high, low = split(x[part])
            y = dot(high, lanes, NT) + dot(low, lanes, NT)
            tiles = [y[r * traj : (r + 1) * traj] for r in range(rows)]
            for j in range(row_bits):
                for r in range(rows):
                    if not r >> j & 1:
                        o = r | 1 << j
                        tiles[r], tiles[o] = swap_lane_bit(tiles[r], tiles[o], j, lane, conditions[j])
            moved.append(jnp.concatenate(tiles))
        y = apply_low(moved, matrices[0])
        work[0] = y[0]
        work[1] = y[1]
        apply_high(work, matrices[1], work)
        y = apply_low([work[0], work[1]], matrices[2])
        if wide:
            y = swap_lane_bit(y[0], y[1], gate_bits - 1, lane)
        sent[cycle, 0] = y[0]
        sent[cycle, 1] = y[1]

    def plan_of(cycle):
        return permutation_plan([perm_ref[cycle, b] for b in range(nbits)], nbits, gate_bits, lane)

    def matrices_of(cycle, plan):
        maps, _ = plan
        return (
            low_matrix(cycle, 0, maps[1]),
            high_matrix(cycle, 1, one_hot(maps[2])),
            low_matrix(cycle, 2, None),
        )

    def view(ref, cycle, block):
        if wide:
            start = pl.multiple_of(block // 2 * traj, traj)
            return ref.at[cycle, pl.ds(block % 2, 1), pl.ds(start, traj), :]
        depth = rows * traj // blocks
        start = pl.multiple_of(block * depth, depth)
        return ref.at[cycle, :, pl.ds(start, depth), :]

    def remote(cycle, step):
        block, to_grp, to_dev, slot = targets(cycle, step)
        return pltpu.make_async_remote_copy(
            src_ref=view(sent, cycle, block),
            dst_ref=view(landed, cycle, slot),
            send_sem=send_sem.at[cycle, step],
            recv_sem=recv_sem.at[cycle, slot],
            device_id=(to_grp, to_dev),
            device_id_type=MESH,
        )

    def stay(cycle):
        block, _, _, slot = targets(cycle, 0)
        return pltpu.make_async_copy(
            view(sent, cycle, block), view(landed, cycle, slot), recv_sem.at[cycle, slot]
        )

    def start(cycle):
        for step in range(blocks - 1, 0, -1):
            remote(cycle, step).start()

        @pl.when(self_sent[cycle])
        def _():
            stay(cycle).start()

        @pl.when(jnp.logical_not(self_sent[cycle]))
        def _():
            remote(cycle, 0).start()

    def finish(cycle):
        for slot in range(blocks):
            pltpu.make_async_copy(
                view(landed, cycle, slot), view(landed, cycle, slot), recv_sem.at[cycle, slot]
            ).wait()

    def finish_sends(cycle):
        for step in range(1, blocks):
            remote(cycle, step).wait_send()

        @pl.when(jnp.logical_not(self_sent[cycle]))
        def _():
            remote(cycle, 0).wait_send()

    def unwiden(cycle):
        if wide:
            y = swap_lane_bit(landed[cycle, 0], landed[cycle, 1], gate_bits - 1, lane)
            landed[cycle, 0] = y[0]
            landed[cycle, 1] = y[1]

    loads[0].wait()
    plan = plan_of(0)
    loads[1].wait()
    x = [
        jnp.concatenate([state_ref[part, :, r * width : (r + 1) * width] for r in range(rows)])
        for part in range(2)
    ]
    local_part(x, plan, 0, matrices_of(0, plan))
    others = 2 * (blocks - 1) + jnp.where(self_sent[0], 0, 1) + jnp.where(self_sent[1], 0, 1)
    pl.semaphore_wait(barrier, others)
    start(0)
    last = high_matrix(0, 3, fixed)
    plan = plan_of(1)
    following = matrices_of(1, plan)
    finish(0)
    unwiden(0)
    apply_high(landed.at[0], last, work)
    local_part([work[0], work[1]], plan, 1, following)
    start(1)
    last = high_matrix(1, 3, fixed)
    finish(1)
    unwiden(1)
    apply_high(landed.at[1], last, work)
    for part in range(2):
        for r in range(rows):
            out_ref[part, :, r * width : (r + 1) * width] = work[part, r * traj : (r + 1) * traj, :]
    finish_sends(0)
    finish_sends(1)


def on_device(state, gates, local_perm):
    traj = state.shape[1]
    nbits = state.shape[2].bit_length() - 1
    gate_bits = gates.shape[-1].bit_length() - 1
    grp_bits = lax.axis_size("grp").bit_length() - 1
    dev_bits = lax.axis_size("dev").bit_length() - 1
    width = 1 << gate_bits
    height = traj << nbits - gate_bits
    vmem = pl.BlockSpec(memory_space=pltpu.VMEM)
    sizes = (traj, nbits, gate_bits, grp_bits, dev_bits)
    return pl.pallas_call(
        functools.partial(kernel, sizes),
        out_shape=jax.ShapeDtypeStruct(state.shape, state.dtype),
        in_specs=[pl.BlockSpec(memory_space=pl.ANY)] * 3,
        out_specs=vmem,
        scratch_shapes=[
            pltpu.VMEM(state.shape, state.dtype),
            pltpu.VMEM(gates.shape, gates.dtype),
            pltpu.SMEM(local_perm.shape, local_perm.dtype),
            pltpu.VMEM((2, height, width), jnp.float32),
            pltpu.VMEM((CYCLES, 2, height, width), jnp.float32),
            pltpu.VMEM((CYCLES, 2, height, width), jnp.float32),
            pltpu.SemaphoreType.DMA((CYCLES, 1 << dev_bits)),
            pltpu.SemaphoreType.DMA((CYCLES, 1 << dev_bits)),
            pltpu.SemaphoreType.DMA((2 + GATES * CYCLES,)),
        ],
        compiler_params=pltpu.CompilerParams(
            collective_id=0, has_side_effects=True, vmem_limit_bytes=32 << 20
        ),
    )(state, gates, local_perm)


def solution(mesh):
    placed = (P(None, None, ("grp", "dev")), P(), P())
    return jax.shard_map(
        on_device,
        mesh=mesh,
        in_specs=placed,
        out_specs=P(None, None, ("grp", "dev")),
        check_vma=False,
    )
```

profile of v0, /device:TPU:0, one launch (start us, length us, event | category | flops | bytes accessed | tf_op | source)
XLA Modules:
  0.0 34.0 jit_solution(1631549351054005200)
XLA Ops:
  0.0 0.0 copy-start
  0.0 1.2 %copy-done = f32[2,4,2,128,128]{4,3,2,1,0:T(8,128)S(1)} copy-done((f32[2,4,2,128,128]{4,3,2,1,0:T(8,128)S(1)}, f32[2,4,2,128,128]{4,3,2,1,0:T(8,128)}, u32[]{:S(2)}) %copy-start) | copy-done | bytes 1048600
  1.2 0.0 copy-start.1
  1.2 0.9 %copy-done.1 = f32[2,8,4096]{2,1,0:T(8,128)S(1)} copy-done((f32[2,8,4096]{2,1,0:T(8,128)S(1)}, f32[2,8,4096]{2,1,0:T(8,128)}, u32[]{:S(2)}) %copy-start.1) | copy-done | bytes 262168
  2.2 0.0 copy-start.2
  2.2 0.7 %copy-done.2 = s32[2,12]{1,0:T(2,128)S(1)} copy-done((s32[2,12]{1,0:T(2,128)S(1)}, s32[2,12]{1,0:T(2,128)}, u32[]{:S(2)}) %copy-start.2) | copy-done | bytes 120
  2.9 30.4 %shard_map.37 = f32[2,8,4096]{2,1,0:T(8,128)S(1)} custom-call(f32[2,8,4096]{2,1,0:T(8,128)S(1)} %copy-done.1, f32[2,4,2,128,128]{4,3,2,1,0:T(8,128)S(1)} %copy-done, s32[2,12]{1,0:T(2,128)S(1)} %copy-done.2), custom_call_target="tpu_custom_call" | custom-call | tf_op jit(solution)/shard_map/pallas_call | solution.py:370
  33.3 0.7 %copy.5 = f32[2,8,4096]{2,1,0:T(8,128)} copy(f32[2,8,4096]{2,1,0:T(8,128)S(1)} %shard_map.37) | data formatting | bytes 524288
Async XLA Ops:
  0.0 1.2 %copy-start = (f32[2,4,2,128,128]{4,3,2,1,0:T(8,128)S(1)}, f32[2,4,2,128,128]{4,3,2,1,0:T(8,128)}, u32[]{:S(2)}) copy-start(f32[2,4,2,128,128]{4,3,2,1,0:T(8,128)} %gates_hbm.1) | copy-start | bytes 3145732
  1.2 0.9 %copy-start.1 = (f32[2,8,4096]{2,1,0:T(8,128)S(1)}, f32[2,8,4096]{2,1,0:T(8,128)}, u32[]{:S(2)}) copy-start(f32[2,8,4096]{2,1,0:T(8,128)} %state_hbm.1) | copy-start | bytes 786436
  2.2 0.7 %copy-start.2 = (s32[2,12]{1,0:T(2,128)S(1)}, s32[2,12]{1,0:T(2,128)}, u32[]{:S(2)}) copy-start(s32[2,12]{1,0:T(2,128)} %perm_hbm.1) | copy-start | bytes 292
where the time goes:
time: 34.2 us; the launch traced here: 34 us
  Pallas kernels  30.4 us (89%)
  local copies, waits for them, and re-layouts  3.56 us (10%)
    pallas_call x1, Pallas kernels, on_device(): pl.pallas_call(functools.partial(kernel, sizes), out_shape=jax.ShapeDtype...  30.4 us
    unnamed x7, local copies, waits for them, and re-layouts  3.56 us

commit v1 on v0

v1 whole, which is shorter than its diff:
```python
import functools

import jax
import jax.numpy as jnp
from jax import lax
from jax.experimental import pallas as pl
from jax.experimental.pallas import tpu as pltpu
from jax.sharding import PartitionSpec as P

MESH = pl.DeviceIdType.MESH
CYCLES = 2
GATES = 4


def permutation_plan(perm, nbits, gate_bits, lane):
    row_bits = nbits - gate_bits
    shared = gate_bits - row_bits
    leaving = sum(1 << perm[b] for b in range(gate_bits, nbits))
    enters = [1 - (leaving >> (gate_bits + j) & 1) for j in range(row_bits)]
    open_slots = closed_slots = 0
    open_at = closed_at = 0
    for j in range(gate_bits):
        is_open = enters[j] if j < row_bits else 0
        open_slots = open_slots + (j * is_open << open_at)
        closed_slots = closed_slots + (j * (1 - is_open) << closed_at)
        open_at = open_at + 4 * is_open
        closed_at = closed_at + 4 * (1 - is_open)
    slot = []
    position_low = position_high = 0
    for q in range(gate_bits):
        leaves = leaving >> q & 1
        here = jnp.where(leaves == 1, open_slots, closed_slots) & 15
        open_slots = open_slots >> 4 * leaves
        closed_slots = closed_slots >> 4 * (1 - leaves)
        slot.append(here)
        position_low = position_low + (here + gate_bits * leaves << 4 * q)
    for j in range(row_bits):
        position_high = position_high + (gate_bits + j - gate_bits * enters[j] << 4 * j)
    placed = []
    for b in range(nbits):
        low = position_low >> 4 * jnp.minimum(perm[b], gate_bits - 1) & 15
        high = position_high >> 4 * jnp.maximum(perm[b] - gate_bits, 0) & 15
        placed.append(jnp.where(perm[b] < gate_bits, low, high))

    def lane_map(places):
        return sum((lane >> k & 1) << place for k, place in enumerate(places))

    high_place = list(range(row_bits, gate_bits)) + [place - gate_bits for place in placed[gate_bits:]]
    maps = [lane_map(slot), lane_map(placed[:gate_bits]), lane_map(high_place)]
    return maps, [enter == 1 for enter in enters]


def split(x):
    high = x.astype(jnp.bfloat16)
    low = (x - high.astype(jnp.float32)).astype(jnp.bfloat16)
    return high, low


def dot(a, b, contract):
    return lax.dot_general(a, b, (contract, ((), ())), preferred_element_type=jnp.float32)


NT = ((1,), (1,))
NN = ((1,), (0,))


def swap_lane_bit(first, second, bit, lane, condition=None):
    width = first.shape[-1]
    axis = first.ndim - 1
    up = (lane >> bit & 1) == 1
    down = ~up
    if condition is not None:
        up = up & condition
        down = down & condition
    new_first = jnp.where(up, pltpu.roll(second, 1 << bit, axis), first)
    new_second = jnp.where(down, pltpu.roll(first, width - (1 << bit), axis), second)
    return new_first, new_second


def one_hot(lane_map):
    width = lane_map.shape[-1]
    rows = lax.broadcasted_iota(jnp.int32, (width, width), 0)
    return jnp.where(rows == lane_map, 1.0, 0.0).astype(jnp.bfloat16)


def stack_parts(real, imag):
    return jnp.concatenate([*split(real), *split(imag)])


def left_matrix(real, imag, columns):
    width = real.shape[-1]
    moved = dot(stack_parts(real, imag), columns, NT).astype(jnp.bfloat16)
    re_high, re_low, im_high, im_low = [moved[i * width : (i + 1) * width] for i in range(4)]

    def whole(re, im):
        return jnp.concatenate(
            [jnp.concatenate([re, -im], axis=1), jnp.concatenate([im, re], axis=1)], axis=0
        )

    return whole(re_high, im_high), whole(re_low, im_low)


def right_matrix(real, imag, columns):
    width = real.shape[-1]
    moved = dot(columns, stack_parts(real, imag), NT).astype(jnp.bfloat16)
    re_high, re_low, im_high, im_low = [moved[:, i * width : (i + 1) * width] for i in range(4)]

    def whole(re, im):
        return jnp.concatenate(
            [jnp.concatenate([re, im], axis=1), jnp.concatenate([-im, re], axis=1)], axis=0
        )

    return whole(re_high, im_high), whole(re_low, im_low)


def kernel(
    sizes,
    state_hbm,
    gates_hbm,
    perm_hbm,
    out_ref,
    state_ref,
    gates_ref,
    perm_ref,
    work,
    final,
    sent,
    landed,
    send_sem,
    recv_sem,
    load_sem,
):
    traj, nbits, gate_bits, dev_bits, halves = sizes
    width = 1 << gate_bits
    row_bits = nbits - gate_bits
    shared = gate_bits - row_bits
    per = 1 << shared
    rows = 1 << row_bits
    blocks = 1 << dev_bits
    top = blocks // 2
    wide = dev_bits > row_bits
    own_traj = traj // halves
    grp = lax.axis_index("grp")
    dev = lax.axis_index("dev")
    grp_low = grp % 2
    grp_next = grp // 2 % 2
    grp_rest = grp // 4 * 4
    dev_top = dev // top
    dev_low = dev % top

    def targets(cycle, step):
        low = (dev_low ^ (step % top)) if step % top else dev_low
        high = 1 - grp_next if step // top else grp_next
        block = high * top + low
        if cycle == 0:
            return block, grp_rest + high * 2 + grp_low, grp_next * top + low, dev
        return block, grp_rest + high * 2 + grp_next, dev_top * top + low, grp_low * top + dev_low

    self_sent = [dev_top == grp_next, grp_low == grp_next]

    barrier = pltpu.get_barrier_semaphore()
    for step in range(blocks):
        low = (dev_low ^ (step % top)) if step % top else dev_low
        high = step // top
        source_high = 1 - dev_top if high else dev_top
        first = (grp_rest + dev_top * 2 + grp_low, source_high * top + low)
        source_low = 1 - grp_low if high else grp_low
        second = (grp_rest + grp_low * 2 + source_low, dev_top * top + low)

        def tell(device):
            pl.semaphore_signal(barrier, inc=1, device_id=device, device_id_type=MESH)

        if step:
            tell(first)
            tell(second)
        else:
            pl.when(dev_top != grp_next)(functools.partial(tell, first))
            pl.when(grp_low != grp_next)(functools.partial(tell, second))

    loads = [
        pltpu.make_async_copy(perm_hbm, perm_ref, load_sem.at[0]),
        pltpu.make_async_copy(state_hbm, state_ref, load_sem.at[1]),
    ]
    for cycle in range(CYCLES):
        for which in range(GATES):
            sem = load_sem.at[2 + GATES * cycle + which]
            loads.append(
                pltpu.make_async_copy(gates_hbm.at[cycle, which], gates_ref.at[cycle, which], sem)
            )
    for load in loads:
        load.start()

    lane = lax.broadcasted_iota(jnp.int32, (1, width), 1)

    def low_matrix(cycle, which, lane_map):
        loads[2 + GATES * cycle + which].wait()
        return right_matrix(gates_ref[cycle, which, 0], gates_ref[cycle, which, 1], one_hot(lane_map))

    def high_matrix(cycle, which, lane_map):
        loads[2 + GATES * cycle + which].wait()
        parts = [
            jnp.concatenate(
                [gates_ref[cycle, which, part, pl.ds(a, rows, stride=per), :] for a in range(per)]
            )
            for part in range(2)
        ]
        return left_matrix(parts[0], parts[1], one_hot(lane_map))

    def plan_of(cycle):
        return permutation_plan([perm_ref[cycle, b] for b in range(nbits)], nbits, gate_bits, lane)

    def matrices_of(cycle, plan):
        maps, _ = plan
        return (
            low_matrix(cycle, 0, maps[1]),
            high_matrix(cycle, 1, maps[2]),
            low_matrix(cycle, 2, lane),
        )

    def last_matrix(cycle):
        return high_matrix(cycle, 3, (lane % per) * rows + lane // per)


    def apply_low(planes, matrix):
        high, low = split(jnp.concatenate([jnp.concatenate(part) for part in planes], axis=1))
        m_high, m_low = matrix
        y = dot(high, m_high, NN) + (dot(low, m_high, NN) + dot(high, m_low, NN))
        return [
            [y[t * rows : (t + 1) * rows, part * width : (part + 1) * width] for t in range(own_traj)]
            for part in range(2)
        ]

    def swap_traj(planes):
        planes = list(planes)
        for bit in range(shared):
            for t in range(len(planes)):
                if not t >> bit & 1:
                    o = t | 1 << bit
                    planes[t], planes[o] = swap_lane_bit(planes[t], planes[o], row_bits + bit, lane)
        return planes

    def apply_high(planes, matrix):
        operand = []
        for part in planes:
            part = swap_traj(part)
            operand.append(
                jnp.concatenate(
                    [jnp.concatenate(part[g : g + per]) for g in range(0, own_traj, per)], axis=1
                )
            )
        high, low = split(jnp.concatenate(operand))
        m_high, m_low = matrix
        y = dot(m_high, high, NN) + (dot(m_low, high, NN) + dot(m_high, low, NN))
        return [
            swap_traj(
                [
                    y[part * width + a * rows : part * width + (a + 1) * rows, g * width : (g + 1) * width]
                    for g in range(own_traj // per)
                    for a in range(per)
                ]
            )
            for part in range(2)
        ]

    def local_part(x, half, cycle, plan, matrices):
        maps, conditions = plan
        lanes = one_hot(maps[0])
        x = jnp.concatenate(split(x), axis=1)
        y = dot(x, jnp.concatenate([lanes, lanes], axis=1), NT)
        height = 2 * own_traj
        tiles = [y[r * height : (r + 1) * height] for r in range(rows)]
        for j in range(row_bits):
            for r in range(rows):
                if not r >> j & 1:
                    o = r | 1 << j
                    tiles[r], tiles[o] = swap_lane_bit(tiles[r], tiles[o], j, lane, conditions[j])
        for r in range(rows):
            work[half, r * height : (r + 1) * height, :] = tiles[r]
        planes = [
            [work[half, pl.ds(part * own_traj + t, rows, stride=height), :] for t in range(own_traj)]
            for part in range(2)
        ]
        planes = apply_low(planes, matrices[0])
        planes = apply_high(planes, matrices[1])
        planes = apply_low(planes, matrices[2])
        if wide:
            pairs = [swap_lane_bit(a, b, gate_bits - 1, lane) for a, b in zip(*planes)]
            planes = list(zip(*pairs))
        for part in range(2):
            for t in range(own_traj):
                sent[cycle, half, part, pl.ds(t, rows, stride=own_traj), :] = planes[part][t]

    def last_part(half, cycle, matrix):
        planes = [
            [landed[cycle, half, part, pl.ds(t, rows, stride=own_traj), :] for t in range(own_traj)]
            for part in range(2)
        ]
        if wide:
            pairs = [swap_lane_bit(a, b, gate_bits - 1, lane) for a, b in zip(*planes)]
            planes = list(zip(*pairs))
        return apply_high(planes, matrix)

    def view(ref, cycle, half, block):
        if wide:
            start = pl.multiple_of(block // 2 * own_traj, own_traj)
            return ref.at[cycle, half, pl.ds(block % 2, 1), pl.ds(start, own_traj), :]
        depth = rows * own_traj // blocks
        start = pl.multiple_of(block * depth, depth)
        return ref.at[cycle, half, :, pl.ds(start, depth), :]

    def remote(cycle, half, step):
        block, to_grp, to_dev, slot = targets(cycle, step)
        return pltpu.make_async_remote_copy(
            src_ref=view(sent, cycle, half, block),
            dst_ref=view(landed, cycle, half, slot),
            send_sem=send_sem.at[cycle, half, step],
            recv_sem=recv_sem.at[cycle, half],
            device_id=(to_grp, to_dev),
            device_id_type=MESH,
        )

    def start(cycle, half):
        for step in range(blocks - 1, 0, -1):
            remote(cycle, half, step).start()

        @pl.when(self_sent[cycle])
        def _():
            block, _, _, slot = targets(cycle, 0)
            pltpu.make_async_copy(
                view(sent, cycle, half, block), view(landed, cycle, half, slot), recv_sem.at[cycle, half]
            ).start()

        @pl.when(jnp.logical_not(self_sent[cycle]))
        def _():
            remote(cycle, half, 0).start()

    def finish(cycle, half):
        whole = landed.at[cycle, half]
        pltpu.make_async_copy(whole, whole, recv_sem.at[cycle, half]).wait()

    def finish_sends(cycle, half):
        for step in range(1, blocks):
            remote(cycle, half, step).wait_send()

        @pl.when(jnp.logical_not(self_sent[cycle]))
        def _():
            remote(cycle, half, 0).wait_send()

    loads[0].wait()
    plan = plan_of(0)
    loads[1].wait()
    matrices = matrices_of(0, plan)
    for half in range(halves):
        tiles = []
        for r in range(rows):
            for part in range(2):
                tiles.append(
                    state_ref[
                        part, half * own_traj : (half + 1) * own_traj, r * width : (r + 1) * width
                    ]
                )
        local_part(jnp.concatenate(tiles), half, 0, plan, matrices)
        if half == 0:
            others = 2 * (blocks - 1) + jnp.where(self_sent[0], 0, 1) + jnp.where(self_sent[1], 0, 1)
            pl.semaphore_wait(barrier, others)
        start(0, half)
    last = last_matrix(0)
    plan = plan_of(1)
    matrices = matrices_of(1, plan)
    for half in range(halves):
        finish(0, half)
        planes = last_part(half, 0, last)
        height = 2 * own_traj
        for part in range(2):
            for t in range(own_traj):
                work[half, pl.ds(part * own_traj + t, rows, stride=height), :] = planes[part][t]
        local_part(work[half], half, 1, plan, matrices)
        start(1, half)
    last = last_matrix(1)
    for half in range(halves):
        finish(1, half)
        planes = last_part(half, 1, last)
        for part in range(2):
            for t in range(own_traj):
                final[part, pl.ds(half * own_traj + t, rows, stride=traj), :] = planes[part][t]
    for part in range(2):
        for r in range(rows):
            out_ref[part, :, r * width : (r + 1) * width] = final[part, r * traj : (r + 1) * traj, :]
    for cycle in range(CYCLES):
        for half in range(halves):
            finish_sends(cycle, half)


def on_device(state, gates, local_perm):
    traj = state.shape[1]
    nbits = state.shape[2].bit_length() - 1
    gate_bits = gates.shape[-1].bit_length() - 1
    dev_bits = lax.axis_size("dev").bit_length() - 1
    width = 1 << gate_bits
    rows = 1 << nbits - gate_bits
    halves = 2 if (rows * traj // 2 >> dev_bits) % 8 == 0 else 1
    sizes = (traj, nbits, gate_bits, dev_bits, halves)
    buffer = pltpu.VMEM((CYCLES, halves, 2, rows * traj // halves, width), jnp.float32)
    return pl.pallas_call(
        functools.partial(kernel, sizes),
        out_shape=jax.ShapeDtypeStruct(state.shape, state.dtype),
        in_specs=[pl.BlockSpec(memory_space=pltpu.HBM)] * 3,
        out_specs=pl.BlockSpec(memory_space=pltpu.VMEM),
        scratch_shapes=[
            pltpu.VMEM(state.shape, state.dtype),
            pltpu.VMEM(gates.shape, gates.dtype),
            pltpu.SMEM(local_perm.shape, local_perm.dtype),
            pltpu.VMEM((halves, 2 * rows * traj // halves, width), jnp.float32),
            pltpu.VMEM((2, rows * traj, width), jnp.float32),
            buffer,
            buffer,
            pltpu.SemaphoreType.DMA((CYCLES, halves, 1 << dev_bits)),
            pltpu.SemaphoreType.DMA((CYCLES, halves)),
            pltpu.SemaphoreType.DMA((2 + GATES * CYCLES,)),
        ],
        compiler_params=pltpu.CompilerParams(
            collective_id=0, has_side_effects=True, vmem_limit_bytes=60 << 20
        ),
    )(state, gates, local_perm)


def solution(mesh):
    placed = (P(None, None, ("grp", "dev")), P(), P())
    return jax.shard_map(
        on_device,
        mesh=mesh,
        in_specs=placed,
        out_specs=P(None, None, ("grp", "dev")),
        check_vma=False,
    )
```

time: 34.2 us -> 29.6 us (0.87)
  Pallas kernels: 30.4 us -> 27.8 us
  local copies, waits for them, and re-layouts: 3.56 us -> 1.67 us
    pallas_call x1, Pallas kernels: 30.4 us -> 27.8 us  [on_device(): pl.pallas_call(functools.partial(kernel, sizes), out_shape=jax.ShapeDtype...]
    unnamed x7 -> x1, local copies, waits for them, and re-layouts: 3.56 us -> 1.67 us
where the time goes in v1:
time: 29.6 us; the launch traced here: 29.4 us
  Pallas kernels  27.8 us (94%)
  local copies, waits for them, and re-layouts  1.67 us (6%)
    pallas_call x1, Pallas kernels, on_device(): pl.pallas_call(functools.partial(kernel, sizes), out_shape=jax.ShapeDtype...  27.8 us
    unnamed x1, local copies, waits for them, and re-layouts  1.67 us

profile of v1, /device:TPU:0, one launch (start us, length us, event | category | flops | bytes accessed | tf_op | source)
XLA Modules:
  0.0 29.4 jit_solution(6724055156626020370)
XLA Ops:
  0.0 27.8 %shard_map.37 = f32[2,8,4096]{2,1,0:T(8,128)} custom-call(f32[2,8,4096]{2,1,0:T(8,128)} %state_hbm.1, f32[2,4,2,128,128]{4,3,2,1,0:T(8,128)} %gates_hbm.1, s32[2,12]{1,0:T(2,128)} %perm_hbm.1), custom_call_target="tpu_custom_call" | custom-call | tf_op jit(solution)/shard_map/pallas_call | solution.py:404
  27.8 1.7 %copy.5 = f32[2,8,4096]{2,1,0:T(8,128)} copy(f32[2,8,4096]{2,1,0:T(8,128)} %shard_map.37) | data formatting | bytes 524288

commit v2 on v1

--- a/solution.py
+++ b/solution.py
@@ -148,24 +148,26 @@
     dev_top = dev // top
     dev_low = dev % top
 
+
     def targets(cycle, step):
         low = (dev_low ^ (step % top)) if step % top else dev_low
-        high = 1 - grp_next if step // top else grp_next
+        own = grp_next if cycle else grp_low
+        high = 1 - own if step // top else own
         block = high * top + low
         if cycle == 0:
-            return block, grp_rest + high * 2 + grp_low, grp_next * top + low, dev
-        return block, grp_rest + high * 2 + grp_next, dev_top * top + low, grp_low * top + dev_low
-
-    self_sent = [dev_top == grp_next, grp_low == grp_next]
+            return block, grp_rest + grp_low * 2 + high, grp_next * top + low, dev
+        return block, grp_rest + high * 2 + grp_low, dev_top * top + low, grp_next * top + dev_low
+
+    stays = jnp.logical_and(grp_low == grp_next, grp_next == dev_top)
 
     barrier = pltpu.get_barrier_semaphore()
     for step in range(blocks):
         low = (dev_low ^ (step % top)) if step % top else dev_low
         high = step // top
-        source_high = 1 - dev_top if high else dev_top
-        first = (grp_rest + dev_top * 2 + grp_low, source_high * top + low)
-        source_low = 1 - grp_low if high else grp_low
-        second = (grp_rest + grp_low * 2 + source_low, dev_top * top + low)
+        source_top = 1 - dev_top if high else dev_top
+        first = (grp_rest + dev_top * 2 + grp_next, source_top * top + low)
+        source_next = 1 - grp_next if high else grp_next
+        second = (grp_rest + source_next * 2 + grp_low, dev_top * top + low)
 
         def tell(device):
             pl.semaphore_signal(barrier, inc=1, device_id=device, device_id_type=MESH)
@@ -174,8 +176,7 @@
             tell(first)
             tell(second)
         else:
-            pl.when(dev_top != grp_next)(functools.partial(tell, first))
-            pl.when(grp_low != grp_next)(functools.partial(tell, second))
+            pl.when(jnp.logical_not(stays))(functools.partial(tell, first))
 
     loads = [
         pltpu.make_async_copy(perm_hbm, perm_ref, load_sem.at[0]),
@@ -323,16 +324,17 @@
         for step in range(blocks - 1, 0, -1):
             remote(cycle, half, step).start()
 
-        @pl.when(self_sent[cycle])
-        def _():
+        def keep():
             block, _, _, slot = targets(cycle, 0)
             pltpu.make_async_copy(
                 view(sent, cycle, half, block), view(landed, cycle, half, slot), recv_sem.at[cycle, half]
             ).start()
 
-        @pl.when(jnp.logical_not(self_sent[cycle]))
-        def _():
-            remote(cycle, half, 0).start()
+        if cycle:
+            keep()
+        else:
+            pl.when(stays)(keep)
+            pl.when(jnp.logical_not(stays))(remote(cycle, half, 0).start)
 
     def finish(cycle, half):
         whole = landed.at[cycle, half]
@@ -342,9 +344,8 @@
         for step in range(1, blocks):
             remote(cycle, half, step).wait_send()
 
-        @pl.when(jnp.logical_not(self_sent[cycle]))
-        def _():
-            remote(cycle, half, 0).wait_send()
+        if not cycle:
+            pl.when(jnp.logical_not(stays))(remote(cycle, half, 0).wait_send)
 
     loads[0].wait()
     plan = plan_of(0)
@@ -361,8 +362,7 @@
                 )
         local_part(jnp.concatenate(tiles), half, 0, plan, matrices)
         if half == 0:
-            others = 2 * (blocks - 1) + jnp.where(self_sent[0], 0, 1) + jnp.where(self_sent[1], 0, 1)
-            pl.semaphore_wait(barrier, others)
+            pl.semaphore_wait(barrier, 2 * (blocks - 1) + jnp.where(stays, 0, 1))
         start(0, half)
     last = last_matrix(0)
     plan = plan_of(1)
@@ -419,9 +419,9 @@
             pltpu.SemaphoreType.DMA((2 + GATES * CYCLES,)),
         ],
         compiler_params=pltpu.CompilerParams(
-            collective_id=0, has_side_effects=True, vmem_limit_bytes=60 << 20
+            collective_id=0, has_side_effects=True, vmem_limit_bytes=32 << 20
         ),
-    )(state, gates, local_perm)
+    )(*[pltpu.with_memory_space_constraint(x, pltpu.HBM) for x in (state, gates, local_perm)])
 
 
 def solution(mesh):

time: 29.6 us -> 26.8 us (0.905)
  Pallas kernels: 27.8 us -> 25.9 us
  local copies, waits for them, and re-layouts: 1.67 us -> 0.71 us
    pallas_call x1, Pallas kernels: 27.8 us -> 25.9 us  [on_device(): pl.pallas_call(functools.partial(kernel, sizes), out_shape=jax.ShapeDtype...]
    unnamed x1, local copies, waits for them, and re-layouts: 1.67 us -> 0.71 us
where the time goes in v2:
time: 26.8 us; the launch traced here: 26.6 us
  Pallas kernels  25.9 us (97%)
  local copies, waits for them, and re-layouts  0.71 us (3%)
    pallas_call x1, Pallas kernels, on_device(): pl.pallas_call(functools.partial(kernel, sizes), out_shape=jax.ShapeDtype...  25.9 us
    unnamed x1, local copies, waits for them, and re-layouts  0.71 us

profile of v2, /device:TPU:0, one launch (start us, length us, event | category | flops | bytes accessed | tf_op | source)
XLA Modules:
  0.0 26.6 jit_solution(793501283734820083)
XLA Ops:
  0.0 25.9 %shard_map.37 = f32[2,8,4096]{2,1,0:T(8,128)S(1)} custom-call(f32[2,8,4096]{2,1,0:T(8,128)} %state_hbm.1, f32[2,4,2,128,128]{4,3,2,1,0:T(8,128)} %gates_hbm.1, s32[2,12]{1,0:T(2,128)} %perm_hbm.1), custom_call_target="tpu_custom_call" | custom-call | tf_op jit(solution)/shard_map/pallas_call | solution.py:404
  25.9 0.7 %copy.5 = f32[2,8,4096]{2,1,0:T(8,128)} copy(f32[2,8,4096]{2,1,0:T(8,128)S(1)} %shard_map.37) | data formatting | bytes 524288

commit v3 on v2

--- a/solution.py
+++ b/solution.py
@@ -126,6 +126,8 @@
     final,
     sent,
     landed,
+    swapped,
+    swap_sem,
     send_sem,
     recv_sem,
     load_sem,
@@ -151,32 +153,35 @@
 
     def targets(cycle, step):
         low = (dev_low ^ (step % top)) if step % top else dev_low
-        own = grp_next if cycle else grp_low
-        high = 1 - own if step // top else own
+        high = 1 - grp_next if step // top else grp_next
         block = high * top + low
         if cycle == 0:
-            return block, grp_rest + grp_low * 2 + high, grp_next * top + low, dev
-        return block, grp_rest + high * 2 + grp_low, dev_top * top + low, grp_next * top + dev_low
-
-    stays = jnp.logical_and(grp_low == grp_next, grp_next == dev_top)
-
+            return block, grp, block, dev
+        return block, grp_rest + high * 2 + grp_next, dev_top * top + low, grp_low * top + dev_low
+
+    def stays(cycle, step):
+        if step % top:
+            return None
+        if cycle == 0:
+            return dev_top != grp_next if step else dev_top == grp_next
+        return None if step else grp_low == grp_next
+
+    other_grp = grp_rest + (1 - grp_next) * 2 + grp_low
     barrier = pltpu.get_barrier_semaphore()
+
+    def tell(device):
+        pl.semaphore_signal(barrier, inc=1, device_id=device, device_id_type=MESH)
+
+    tell((other_grp, dev))
     for step in range(blocks):
         low = (dev_low ^ (step % top)) if step % top else dev_low
-        high = step // top
-        source_top = 1 - dev_top if high else dev_top
-        first = (grp_rest + dev_top * 2 + grp_next, source_top * top + low)
-        source_next = 1 - grp_next if high else grp_next
-        second = (grp_rest + source_next * 2 + grp_low, dev_top * top + low)
-
-        def tell(device):
-            pl.semaphore_signal(barrier, inc=1, device_id=device, device_id_type=MESH)
-
         if step:
-            tell(first)
-            tell(second)
+            tell((grp, (1 - dev_top if step // top else dev_top) * top + low))
+        source = (grp_rest + grp_low * 2 + (1 - grp_low if step // top else grp_low), dev_top * top + low)
+        if step:
+            tell(source)
         else:
-            pl.when(jnp.logical_not(stays))(functools.partial(tell, first))
+            pl.when(grp_low != grp_next)(functools.partial(tell, source))
 
     loads = [
         pltpu.make_async_copy(perm_hbm, perm_ref, load_sem.at[0]),
@@ -309,10 +314,27 @@
         start = pl.multiple_of(block * depth, depth)
         return ref.at[cycle, half, :, pl.ds(start, depth), :]
 
+    def source_of(cycle, half, step, block):
+        if cycle == 0 and step // top:
+            return view(swapped, 0, half, block % top)
+        return view(sent, cycle, half, block)
+
+    def swap(half):
+        size = rows * own_traj // 2
+        start = pl.multiple_of((1 - grp_next) * size, size)
+        return pltpu.make_async_remote_copy(
+            src_ref=sent.at[0, half, :, pl.ds(start, size), :],
+            dst_ref=swapped.at[0, half],
+            send_sem=swap_sem.at[0, half],
+            recv_sem=swap_sem.at[1, half],
+            device_id=(other_grp, dev),
+            device_id_type=MESH,
+        )
+
     def remote(cycle, half, step):
         block, to_grp, to_dev, slot = targets(cycle, step)
         return pltpu.make_async_remote_copy(
-            src_ref=view(sent, cycle, half, block),
+            src_ref=source_of(cycle, half, step, block),
             dst_ref=view(landed, cycle, half, slot),
             send_sem=send_sem.at[cycle, half, step],
             recv_sem=recv_sem.at[cycle, half],
@@ -320,32 +342,35 @@
             device_id_type=MESH,
         )
 
-    def start(cycle, half):
-        for step in range(blocks - 1, 0, -1):
-            remote(cycle, half, step).start()
-
-        def keep():
-            block, _, _, slot = targets(cycle, 0)
-            pltpu.make_async_copy(
-                view(sent, cycle, half, block), view(landed, cycle, half, slot), recv_sem.at[cycle, half]
-            ).start()
-
-        if cycle:
-            keep()
-        else:
-            pl.when(stays)(keep)
-            pl.when(jnp.logical_not(stays))(remote(cycle, half, 0).start)
+    def start(cycle, half, steps):
+        for step in reversed(steps):
+            own = stays(cycle, step)
+            if own is None:
+                remote(cycle, half, step).start()
+                continue
+
+            def keep():
+                block, _, _, slot = targets(cycle, step)
+                pltpu.make_async_copy(
+                    source_of(cycle, half, step, block),
+                    view(landed, cycle, half, slot),
+                    recv_sem.at[cycle, half],
+                ).start()
+
+            pl.when(own)(keep)
+            pl.when(jnp.logical_not(own))(remote(cycle, half, step).start)
 
     def finish(cycle, half):
         whole = landed.at[cycle, half]
         pltpu.make_async_copy(whole, whole, recv_sem.at[cycle, half]).wait()
 
     def finish_sends(cycle, half):
-        for step in range(1, blocks):
-            remote(cycle, half, step).wait_send()
-
-        if not cycle:
-            pl.when(jnp.logical_not(stays))(remote(cycle, half, 0).wait_send)
+        for step in range(blocks):
+            own = stays(cycle, step)
+            if own is None:
+                remote(cycle, half, step).wait_send()
+            else:
+                pl.when(jnp.logical_not(own))(remote(cycle, half, step).wait_send)
 
     loads[0].wait()
     plan = plan_of(0)
@@ -362,8 +387,12 @@
                 )
         local_part(jnp.concatenate(tiles), half, 0, plan, matrices)
         if half == 0:
-            pl.semaphore_wait(barrier, 2 * (blocks - 1) + jnp.where(stays, 0, 1))
-        start(0, half)
+            pl.semaphore_wait(barrier, 2 * blocks - 1 + jnp.where(grp_low == grp_next, 0, 1))
+        swap(half).start()
+        start(0, half, range(top))
+    for half in range(halves):
+        swap(half).wait_recv()
+        start(0, half, range(top, blocks))
     last = last_matrix(0)
     plan = plan_of(1)
     matrices = matrices_of(1, plan)
@@ -375,7 +404,7 @@
             for t in range(own_traj):
                 work[half, pl.ds(part * own_traj + t, rows, stride=height), :] = planes[part][t]
         local_part(work[half], half, 1, plan, matrices)
-        start(1, half)
+        start(1, half, range(blocks))
     last = last_matrix(1)
     for half in range(halves):
         finish(1, half)
@@ -386,6 +415,8 @@
     for part in range(2):
         for r in range(rows):
             out_ref[part, :, r * width : (r + 1) * width] = final[part, r * traj : (r + 1) * traj, :]
+    for half in range(halves):
+        swap(half).wait_send()
     for cycle in range(CYCLES):
         for half in range(halves):
             finish_sends(cycle, half)
@@ -414,6 +445,8 @@
             pltpu.VMEM((2, rows * traj, width), jnp.float32),
             buffer,
             buffer,
+            pltpu.VMEM((1, halves, 2, rows * traj // halves // 2, width), jnp.float32),
+            pltpu.SemaphoreType.DMA((2, halves)),
             pltpu.SemaphoreType.DMA((CYCLES, halves, 1 << dev_bits)),
             pltpu.SemaphoreType.DMA((CYCLES, halves)),
             pltpu.SemaphoreType.DMA((2 + GATES * CYCLES,)),

time: 26.8 us -> 24.1 us (0.90)
  the two profiles are of different devices: /device:TPU:0 before, /device:TPU:2 now
where the time goes in v3:
time: 24.1 us; the launch traced here: 24 us
  Pallas kernels  23.3 us (97%)
  local copies, waits for them, and re-layouts  0.71 us (3%)
    pallas_call x1, Pallas kernels, on_device(): pl.pallas_call(functools.partial(kernel, sizes), out_shape=jax.ShapeDtype...  23.3 us
    unnamed x1, local copies, waits for them, and re-layouts  0.71 us

profile of v3, /device:TPU:2, one launch (start us, length us, event | category | flops | bytes accessed | tf_op | source)
XLA Modules:
  0.0 24.0 jit_solution(17015492156503379721)
XLA Ops:
  0.0 23.3 %shard_map.37 = f32[2,8,4096]{2,1,0:T(8,128)S(1)} custom-call(f32[2,8,4096]{2,1,0:T(8,128)} %state_hbm.1, f32[2,4,2,128,128]{4,3,2,1,0:T(8,128)} %gates_hbm.1, s32[2,12]{1,0:T(2,128)} %perm_hbm.1), custom_call_target="tpu_custom_call" | custom-call | tf_op jit(solution)/shard_map/pallas_call | solution.py:435
  23.3 0.7 %copy.5 = f32[2,8,4096]{2,1,0:T(8,128)} copy(f32[2,8,4096]{2,1,0:T(8,128)S(1)} %shard_map.37) | data formatting | bytes 524288

commit v4 on v3

--- a/solution.py
+++ b/solution.py
@@ -97,7 +97,8 @@
             [jnp.concatenate([re, -im], axis=1), jnp.concatenate([im, re], axis=1)], axis=0
         )
 
-    return whole(re_high, im_high), whole(re_low, im_low)
+    high, low = whole(re_high, im_high), whole(re_low, im_low)
+    return jnp.concatenate([high, low, high], axis=1)
 
 
 def right_matrix(real, imag, columns):
@@ -110,7 +111,8 @@
             [jnp.concatenate([re, im], axis=1), jnp.concatenate([-im, re], axis=1)], axis=0
         )
 
-    return whole(re_high, im_high), whole(re_low, im_low)
+    high, low = whole(re_high, im_high), whole(re_low, im_low)
+    return jnp.concatenate([high, low, high], axis=0)
 
 
 def kernel(
@@ -166,23 +168,6 @@
             return dev_top != grp_next if step else dev_top == grp_next
         return None if step else grp_low == grp_next
 
-    other_grp = grp_rest + (1 - grp_next) * 2 + grp_low
-    barrier = pltpu.get_barrier_semaphore()
-
-    def tell(device):
-        pl.semaphore_signal(barrier, inc=1, device_id=device, device_id_type=MESH)
-
-    tell((other_grp, dev))
-    for step in range(blocks):
-        low = (dev_low ^ (step % top)) if step % top else dev_low
-        if step:
-            tell((grp, (1 - dev_top if step // top else dev_top) * top + low))
-        source = (grp_rest + grp_low * 2 + (1 - grp_low if step // top else grp_low), dev_top * top + low)
-        if step:
-            tell(source)
-        else:
-            pl.when(grp_low != grp_next)(functools.partial(tell, source))
-
     loads = [
         pltpu.make_async_copy(perm_hbm, perm_ref, load_sem.at[0]),
         pltpu.make_async_copy(state_hbm, state_ref, load_sem.at[1]),
@@ -196,6 +181,23 @@
     for load in loads:
         load.start()
 
+    other_grp = grp_rest + (1 - grp_next) * 2 + grp_low
+    barrier = pltpu.get_barrier_semaphore()
+
+    def tell(device):
+        pl.semaphore_signal(barrier, inc=1, device_id=device, device_id_type=MESH)
+
+    tell((other_grp, dev))
+    for step in range(blocks):
+        low = (dev_low ^ (step % top)) if step % top else dev_low
+        if step:
+            tell((grp, (1 - dev_top if step // top else dev_top) * top + low))
+        source = (grp_rest + grp_low * 2 + (1 - grp_low if step // top else grp_low), dev_top * top + low)
+        if step:
+            tell(source)
+        else:
+            pl.when(grp_low != grp_next)(functools.partial(tell, source))
+
     lane = lax.broadcasted_iota(jnp.int32, (1, width), 1)
 
     def low_matrix(cycle, which, lane_map):
@@ -229,8 +231,7 @@
 
     def apply_low(planes, matrix):
         high, low = split(jnp.concatenate([jnp.concatenate(part) for part in planes], axis=1))
-        m_high, m_low = matrix
-        y = dot(high, m_high, NN) + (dot(low, m_high, NN) + dot(high, m_low, NN))
+        y = dot(jnp.concatenate([high, high, low], axis=1), matrix, NN)
         return [
             [y[t * rows : (t + 1) * rows, part * width : (part + 1) * width] for t in range(own_traj)]
             for part in range(2)
@@ -255,8 +256,7 @@
                 )
             )
         high, low = split(jnp.concatenate(operand))
-        m_high, m_low = matrix
-        y = dot(m_high, high, NN) + (dot(m_low, high, NN) + dot(m_high, low, NN))
+        y = dot(matrix, jnp.concatenate([high, high, low]), NN)
         return [
             swap_traj(
                 [

time: 24.1 us -> 24.1 us (level)
  no operation moved by 1% of the time
where the time goes in v4:
time: 24.1 us; the launch traced here: 23.9 us
  Pallas kernels  23.2 us (96%)
  local copies, waits for them, and re-layouts  0.71 us (3%)
    pallas_call x1, Pallas kernels, on_device(): pl.pallas_call(functools.partial(kernel, sizes), out_shape=jax.ShapeDtype...  23.2 us
    unnamed x1, local copies, waits for them, and re-layouts  0.71 us

profile of v4, /device:TPU:2, one launch (start us, length us, event | category | flops | bytes accessed | tf_op | source)
XLA Modules:
  0.0 23.9 jit_solution(14647061529060302014)
XLA Ops:
  0.0 23.2 %shard_map.37 = f32[2,8,4096]{2,1,0:T(8,128)S(1)} custom-call(f32[2,8,4096]{2,1,0:T(8,128)} %state_hbm.1, f32[2,4,2,128,128]{4,3,2,1,0:T(8,128)} %gates_hbm.1, s32[2,12]{1,0:T(2,128)} %perm_hbm.1), custom_call_target="tpu_custom_call" | custom-call | tf_op jit(solution)/shard_map/pallas_call | solution.py:435
  23.2 0.7 %copy.5 = f32[2,8,4096]{2,1,0:T(8,128)} copy(f32[2,8,4096]{2,1,0:T(8,128)S(1)} %shard_map.37) | data formatting | bytes 524288

commit v5 on v4

--- a/solution.py
+++ b/solution.py
@@ -319,14 +319,13 @@
             return view(swapped, 0, half, block % top)
         return view(sent, cycle, half, block)
 
-    def swap(half):
-        size = rows * own_traj // 2
-        start = pl.multiple_of((1 - grp_next) * size, size)
+    def swap(half, step):
+        low = (dev_low ^ step) if step else dev_low
         return pltpu.make_async_remote_copy(
-            src_ref=sent.at[0, half, :, pl.ds(start, size), :],
-            dst_ref=swapped.at[0, half],
-            send_sem=swap_sem.at[0, half],
-            recv_sem=swap_sem.at[1, half],
+            src_ref=view(sent, 0, half, (1 - grp_next) * top + low),
+            dst_ref=view(swapped, 0, half, low),
+            send_sem=swap_sem.at[0, half, step],
+            recv_sem=swap_sem.at[1, half, step],
             device_id=(other_grp, dev),
             device_id_type=MESH,
         )
@@ -388,11 +387,13 @@
         local_part(jnp.concatenate(tiles), half, 0, plan, matrices)
         if half == 0:
             pl.semaphore_wait(barrier, 2 * blocks - 1 + jnp.where(grp_low == grp_next, 0, 1))
-        swap(half).start()
+        for step in reversed(range(top)):
+            swap(half, step).start()
         start(0, half, range(top))
     for half in range(halves):
-        swap(half).wait_recv()
-        start(0, half, range(top, blocks))
+        for step in reversed(range(top)):
+            swap(half, step).wait_recv()
+            start(0, half, [top + step])
     last = last_matrix(0)
     plan = plan_of(1)
     matrices = matrices_of(1, plan)
@@ -416,7 +417,8 @@
         for r in range(rows):
             out_ref[part, :, r * width : (r + 1) * width] = final[part, r * traj : (r + 1) * traj, :]
     for half in range(halves):
-        swap(half).wait_send()
+        for step in range(top):
+            swap(half, step).wait_send()
     for cycle in range(CYCLES):
         for half in range(halves):
             finish_sends(cycle, half)
@@ -446,7 +448,7 @@
             buffer,
             buffer,
             pltpu.VMEM((1, halves, 2, rows * traj // halves // 2, width), jnp.float32),
-            pltpu.SemaphoreType.DMA((2, halves)),
+            pltpu.SemaphoreType.DMA((2, halves, 1 << dev_bits - 1)),
             pltpu.SemaphoreType.DMA((CYCLES, halves, 1 << dev_bits)),
             pltpu.SemaphoreType.DMA((CYCLES, halves)),
             pltpu.SemaphoreType.DMA((2 + GATES * CYCLES,)),

time: 24.1 us -> 24.5 us (1.017)
  the two profiles are of different devices: /device:TPU:2 before, /device:TPU:3 now
where the time goes in v5:
time: 24.5 us; the launch traced here: 24.3 us
  Pallas kernels  23.6 us (96%)
  local copies, waits for them, and re-layouts  0.71 us (3%)
    pallas_call x1, Pallas kernels, on_device(): pl.pallas_call(functools.partial(kernel, sizes), out_shape=jax.ShapeDtype...  23.6 us
    unnamed x1, local copies, waits for them, and re-layouts  0.71 us

profile of v5, /device:TPU:3, one launch (start us, length us, event | category | flops | bytes accessed | tf_op | source)
XLA Modules:
  0.0 24.3 jit_solution(15414424132679130147)
XLA Ops:
  0.0 23.6 %shard_map.37 = f32[2,8,4096]{2,1,0:T(8,128)S(1)} custom-call(f32[2,8,4096]{2,1,0:T(8,128)} %state_hbm.1, f32[2,4,2,128,128]{4,3,2,1,0:T(8,128)} %gates_hbm.1, s32[2,12]{1,0:T(2,128)} %perm_hbm.1), custom_call_target="tpu_custom_call" | custom-call | tf_op jit(solution)/shard_map/pallas_call | solution.py:437
  23.6 0.7 %copy.5 = f32[2,8,4096]{2,1,0:T(8,128)} copy(f32[2,8,4096]{2,1,0:T(8,128)S(1)} %shard_map.37) | data formatting | bytes 524288
